TPU v7x, 128 devices: a whole 4x4x4 slice. The times are simulated.
128 devices in a mesh: pair: 8 (over z_lo, x), tile: 16 (over z_hi, y, core).
Axes of the slice: x: 4, y: 4, z: 4 (z_hi: 2, z_lo: 2; z = z_hi * 2 + z_lo), core: 2. Of those that a mesh axis runs over, the one named last changes fastest.
Arguments:
- wrapped: bfloat16 [512, 256, 512], P(None, ('tile', 'pair')), may hold values from -6 to 6
- projector: bfloat16 [512, 512], replicated, may hold values from -1 to 1
- cycles_down: int32 [256, 512], P('tile'), may hold values from -1 to 1
- cycles_across: int32 [256, 512], P('tile'), may hold values from -1 to 1
- weight_class: int32 [256, 512], P('tile'), may hold values from 0 to 3
Outputs:
- unwrapped: float32 [512, 256, 512], P('pair', 'tile')
- misfit: float32 [512, 256, 512], P(None, ('tile', 'pair'))
All inputs are finite; a program needn't handle non-finite values.
Results may differ from a plain program's by a relative error of at most 0.0037.
Values may be sent and summed in bfloat16 or wider, within the bound.
No kernel may reach another device: no remote copies, remote signals or barrier semaphores. Data moves between devices by JAX's collectives and lax.ppermute only.
A program may use at most 64 MiB of HBM per device.

v0:
```python
import functools

import jax
import jax.numpy as jnp
from jax import lax
from jax.experimental import pallas as pl
from jax.experimental.pallas import tpu as pltpu
from jax.sharding import PartitionSpec as P

TEMP_ITERS = 6
SWEEPS = 8


SHRINK = 0.5
DUAL_STEP = 0.35
PRIMAL_STEP = 0.35
FIDELITY = 0.5
LEVELS = (0.25, 0.5, 1.0, 2.0)

HALO = 8
LANES = 128
VMEM_LIMIT = 40 * 2**20


def clip(value, bound):
    return jnp.minimum(jnp.maximum(value, -bound), bound)


def temporal_kernel(wrapped_ref, projector_ref, estimate_ref, misfit_ref, phases_ref, multiplier_ref):
    pairs = projector_ref.shape[0]
    per_pair = wrapped_ref.shape[0] // pairs
    peers, rows, group, _ = estimate_ref.shape
    pieces, _, width = multiplier_ref.shape
    wide = width // LANES

    def parts_of(piece):
        return range(piece * wide, (piece + 1) * wide)

    phases_ref[...] = wrapped_ref[...].astype(jnp.float32)
    projector = projector_ref[...]

    def phases_of(piece):
        return jnp.concatenate([phases_ref[pl.ds(k, pairs, stride=per_pair), :] for k in parts_of(piece)], axis=1)

    blended = [phases_of(piece).astype(jnp.bfloat16) for piece in range(pieces)]
    for iteration in range(TEMP_ITERS):
        for piece in range(pieces):
            mapped = jnp.dot(projector, blended[piece], preferred_element_type=jnp.float32)
            carried = mapped if iteration == 0 else mapped + multiplier_ref[piece]
            excess = carried - phases_of(piece)
            multiplier = clip(excess, SHRINK)
            if iteration < TEMP_ITERS - 1:
                multiplier_ref[piece] = multiplier
                blended[piece] = (carried - 2.0 * multiplier).astype(jnp.bfloat16)
                continue
            misfit = excess - multiplier
            estimate = mapped.astype(jnp.bfloat16)
            for at, k in enumerate(parts_of(piece)):
                columns = slice(at * LANES, (at + 1) * LANES)
                misfit_ref[pl.ds(k, pairs, stride=per_pair), :] = misfit[:, columns]
                tile, row = divmod(k, rows)
                for peer in range(peers):
                    estimate_ref[peer, row, :, tile * LANES : (tile + 1) * LANES] = estimate[
                        peer * group : (peer + 1) * group, columns
                    ]


def temporal_section(wrapped, projector, peers):
    pairs, rows, columns = wrapped.shape
    tiles = columns // LANES
    flat = wrapped.reshape(pairs, rows, tiles, LANES).transpose(0, 2, 1, 3).reshape(-1, LANES)
    in_vmem = pl.BlockSpec(memory_space=pltpu.VMEM)
    width = 2 * LANES
    pieces = rows * columns // width
    estimate, misfit = pl.pallas_call(
        temporal_kernel,
        out_shape=(
            jax.ShapeDtypeStruct((peers, rows, pairs // peers, columns), jnp.bfloat16),
            jax.ShapeDtypeStruct(flat.shape, jnp.float32),
        ),
        in_specs=[in_vmem, in_vmem],
        out_specs=(in_vmem, in_vmem),
        scratch_shapes=[pltpu.VMEM(flat.shape, jnp.float32), pltpu.VMEM((pieces, pairs, width), jnp.float32)],
        compiler_params=pltpu.CompilerParams(vmem_limit_bytes=VMEM_LIMIT),
        cost_estimate=pl.CostEstimate(
            flops=2 * TEMP_ITERS * pairs * pairs * rows * columns, bytes_accessed=4 * 2**20, transcendentals=0
        ),
    )(flat, projector)
    misfit = misfit.reshape(pairs, tiles, rows, LANES).transpose(0, 2, 1, 3).reshape(pairs, rows, columns)
    return estimate, misfit


def deviation_kernel(above_ref, own_ref, below_ref, deviation_ref):
    def extended(at):
        return jnp.concatenate([ref[at] for ref in (above_ref, own_ref, below_ref)], axis=0).astype(jnp.float32)

    cycles_down, cycles_across, classes = extended(0), extended(1), extended(2)
    rows, columns = classes.shape
    limits = jnp.zeros(classes.shape, jnp.float32)
    for number, level in enumerate(LEVELS):
        limits = limits + jnp.where(classes == number + 1, level, 0.0)
    is_last = lax.broadcasted_iota(jnp.int32, classes.shape, 1) == columns - 1
    limits_across = jnp.where(is_last, 0.0, limits)
    limits_down = jnp.where(pltpu.roll(classes, rows - 1, 0) == 0, 0.0, limits)
    step_down, step_across = DUAL_STEP * cycles_down, DUAL_STEP * cycles_across
    shrink = 1.0 / (1.0 + PRIMAL_STEP * FIDELITY)

    zero = jnp.zeros(classes.shape, jnp.float32)
    deviation, deviation_bar, dual_down, dual_across = zero, zero, zero, zero
    for _ in range(SWEEPS):
        down = pltpu.roll(deviation_bar, rows - 1, 0) - deviation_bar
        across = pltpu.roll(deviation_bar, columns - 1, 1) - deviation_bar
        dual_down = clip(dual_down + DUAL_STEP * down - step_down, limits_down)
        dual_across = clip(dual_across + DUAL_STEP * across - step_across, limits_across)
        diverge = dual_down - pltpu.roll(dual_down, 1, 0) + dual_across - pltpu.roll(dual_across, 1, 1)
        updated = (deviation + PRIMAL_STEP * diverge) * shrink
        deviation_bar = 2.0 * updated - deviation
        deviation = updated
    deviation_ref[...] = deviation[HALO : HALO + deviation_ref.shape[0]]


def shifted(value, axis, by):
    peers = lax.axis_size(axis)
    pairs = [(i, i + by) for i in range(peers) if 0 <= i + by < peers]
    return lax.ppermute(value, axis, pairs)


def deviation_section(cycles_down, cycles_across, weight_class):
    own = jnp.stack([cycles_down, cycles_across, weight_class + 1])
    above = shifted(own[:, -HALO:], "tile", 1)
    below = shifted(own[:, :HALO], "tile", -1)
    in_vmem = pl.BlockSpec(memory_space=pltpu.VMEM)
    return pl.pallas_call(
        deviation_kernel,
        out_shape=jax.ShapeDtypeStruct(cycles_down.shape, jnp.float32),
        in_specs=[in_vmem] * 3,
        out_specs=in_vmem,
        compiler_params=pltpu.CompilerParams(vmem_limit_bytes=8 * 2**20),
        cost_estimate=pl.CostEstimate(flops=4 * 2**20, bytes_accessed=2**18, transcendentals=0),
    )(above, own, below)


def combine_kernel(order_ref, estimate_ref, deviation_ref, unwrapped_ref):
    rows, group, columns = estimate_ref.shape
    turned = jnp.dot(
        order_ref[...], estimate_ref[...].reshape(rows * group, columns), preferred_element_type=jnp.float32
    )
    unwrapped_ref[...] = turned.reshape(group, rows, columns) + deviation_ref[...][None]


def combine(estimate, deviation):
    rows, pairs, columns = estimate.shape
    group = 16
    size = rows * group
    place = jnp.arange(size)
    source = place % rows * group + place // rows
    order = (source[:, None] == place[None]).astype(jnp.bfloat16)
    return pl.pallas_call(
        combine_kernel,
        grid=(pairs // group,),
        out_shape=jax.ShapeDtypeStruct((pairs, rows, columns), jnp.float32),
        in_specs=[
            pl.BlockSpec((size, size), lambda i: (0, 0)),
            pl.BlockSpec((rows, group, columns), lambda i: (0, i, 0)),
            pl.BlockSpec((rows, columns), lambda i: (0, 0)),
        ],
        out_specs=pl.BlockSpec((group, rows, columns), lambda i: (i, 0, 0)),
        compiler_params=pltpu.CompilerParams(vmem_limit_bytes=16 * 2**20),
    )(order, estimate, deviation)


def per_device(wrapped, projector, cycles_down, cycles_across, weight_class):
    estimate, misfit = temporal_section(wrapped, projector, lax.axis_size("pair"))
    moved = lax.all_to_all(estimate, "pair", split_axis=0, concat_axis=0, tiled=True)
    deviation = deviation_section(cycles_down, cycles_across, weight_class)
    peers, rows, group, columns = moved.shape
    unwrapped = combine(moved.reshape(peers * rows, group, columns), deviation)
    return unwrapped, misfit


def solution(mesh):
    placed = (
        P(None, ("tile", "pair"), None),
        P(),
        P("tile", None),
        P("tile", None),
        P("tile", None),
    )
    return jax.shard_map(
        per_device,
        mesh=mesh,
        in_specs=placed,
        out_specs=(P("pair", "tile", None), P(None, ("tile", "pair"), None)),
        check_vma=False,
    )
```

profile of v0, /device:TPU:1, one launch (start us, length us, event | category | flops | bytes accessed | tf_op | source)
XLA Modules:
  0.0 35.1 jit_solution(6925603074188977204)
XLA Ops:
  0.6 0.0 copy-start
  0.6 1.2 %copy-done = bf16[512,2,512]{2,1,0:T(2,128)(2,1)S(1)} copy-done((bf16[512,2,512]{2,1,0:T(2,128)(2,1)S(1)}, bf16[512,2,512]{2,1,0:T(2,128)(2,1)}, u32[]{:S(2)}) %copy-start) | copy-done | bytes 1048600
  1.9 0.0 copy-start.1
  1.9 1.0 %copy-done.1 = bf16[512,512]{1,0:T(8,128)(2,1)S(1)} copy-done((bf16[512,512]{1,0:T(8,128)(2,1)S(1)}, bf16[512,512]{1,0:T(8,128)(2,1)}, u32[]{:S(2)}) %copy-start.1) | copy-done | bytes 524312
  2.9 7.4 %shard_map.68 = (bf16[8,2,64,512]{3,2,1,0:T(8,128)(2,1)}, f32[4096,128]{1,0:T(8,128)}) custom-call(bf16[4096,128]{1,0:T(8,128)(2,1)S(1)} %bitcast.16, bf16[512,512]{1,0:T(8,128)(2,1)S(1)} %copy-done.1), custom_call_target="tpu_custom_call" | custom-call | flops 3221225472 | bytes 4194304 | tf_op jit(solution)/shard_map/pallas_call | solution.py:75
  10.3 0.0 copy-start.2
  10.3 0.0 copy-start.3
  10.3 0.0 copy-start.4
  10.3 6.3 %all-to-all-start = ((bf16[8,2,64,512]{3,2,1,0:T(8,128)(2,1)}), bf16[8,2,64,512]{3,2,1,0:T(8,128)(2,1)S(1)}, u32[]{:S(2)}, u32[]{:S(2)}) async-start(bf16[8,2,64,512]{3,2,1,0:T(8,128)(2,1)} %get-tuple-element.4), calls=%async_computation | async-start | bytes 2097152 | tf_op jit(solution)/shard_map/all_to_all | solution.py:174
  16.7 0.0 copy-done.2
  16.7 0.0 copy-done.3
  16.7 0.0 copy-done.4
  16.7 2.9 %collective-permute-start.1 = (s32[3,8,512]{2,1,0:T(8,128)S(1)}, s32[3,8,512]{2,1,0:T(8,128)S(1)}, u32[]{:S(2)}, u32[]{:S(2)}) collective-permute-start(s32[3,8,512]{2,1,0:T(8,128)S(1)} %get-tuple-element.6), channel_id=1, source_target_pairs={{1,0},{2,1},{3,2},{4,3},{5,4},{6,5},{7,6},{8,7},{9,8},{10,9},{11,1... | collective-permute-start | bytes 147464 | tf_op jit(solution)/shard_map/ppermute | solution.py:125
  19.6 3.1 %collective-permute-start = (s32[3,8,512]{2,1,0:T(8,128)S(1)}, s32[3,8,512]{2,1,0:T(8,128)S(1)}, u32[]{:S(2)}, u32[]{:S(2)}) collective-permute-start(s32[3,8,512]{2,1,0:T(8,128)S(1)} %get-tuple-element.7), channel_id=1, source_target_pairs={{0,1},{1,2},{2,3},{3,4},{4,5},{5,6},{6,7},{7,8},{8,9},{9,10},{10,1... | collective-permute-start | bytes 147464 | tf_op jit(solution)/shard_map/ppermute | solution.py:125
  22.7 0.1 fusion.order_ref
  22.8 0.0 collective-permute-done.1.below_ref
  22.8 1.0 %collective-permute-done.above_ref = s32[3,8,512]{2,1,0:T(8,128)S(1)} collective-permute-done((s32[3,8,512]{2,1,0:T(8,128)S(1)}, s32[3,8,512]{2,1,0:T(8,128)S(1)}, u32[]{:S(2)}, u32[]{:S(2)}) %collective-permute-start) | collective-permute-done | bytes 49184 | tf_op jit(solution)/shard_map/ppermute | solution.py:125
  23.9 1.3 %shard_map.69.deviation_ref = f32[16,512]{1,0:T(8,128)S(1)} custom-call(s32[3,8,512]{2,1,0:T(8,128)S(1)} %collective-permute-done.above_ref, s32[3,16,512]{2,1,0:T(8,128)S(1)} %pad_add_fusion.own_ref, s32[3,8,512]{2,1,0:T(8,128)S(1)} %collective-permute-done.1.below_ref), custom_call_target="tpu_custom_call" | custom-call | flops 4194304 | bytes 262144 | tf_op jit(solution)/shard_map/pallas_call | solution.py:133
  25.1 7.6 %all-to-all-done = bf16[8,2,64,512]{3,2,1,0:T(8,128)(2,1)S(1)} async-done(((bf16[8,2,64,512]{3,2,1,0:T(8,128)(2,1)}), bf16[8,2,64,512]{3,2,1,0:T(8,128)(2,1)S(1)}, u32[]{:S(2)}, u32[]{:S(2)}) %all-to-all-start) | async-done | bytes 1048608 | tf_op jit(solution)/shard_map/all_to_all | solution.py:174
  32.7 2.4 %shard_map.70 = f32[64,16,512]{2,1,0:T(8,128)} custom-call(bf16[256,256]{1,0:T(8,128)(2,1)S(1)} %fusion.order_ref, bf16[16,64,512]{2,1,0:T(8,128)(2,1)S(1)} %bitcast.15, f32[16,512]{1,0:T(8,128)S(1)} %shard_map.69.deviation_ref), custom_call_target="tpu_custom_call" | custom-call | tf_op jit(solution)/shard_map/pallas_call | solution.py:158
  (4 shorter events, 0.0 us)
Async XLA Ops:
  0.6 1.2 %copy-start = (bf16[512,2,512]{2,1,0:T(2,128)(2,1)S(1)}, bf16[512,2,512]{2,1,0:T(2,128)(2,1)}, u32[]{:S(2)}) copy-start(bf16[512,2,512]{2,1,0:T(2,128)(2,1)} %param.5) | copy-start | bytes 3145732
  1.9 1.0 %copy-start.1 = (bf16[512,512]{1,0:T(8,128)(2,1)S(1)}, bf16[512,512]{1,0:T(8,128)(2,1)}, u32[]{:S(2)}) copy-start(bf16[512,512]{1,0:T(8,128)(2,1)} %projector_ref.1) | copy-start | bytes 1572868
  10.3 6.3 %copy-start.2 = (s32[16,512]{1,0:T(8,128)S(1)}, s32[16,512]{1,0:T(8,128)}, u32[]{:S(2)}) copy-start(s32[16,512]{1,0:T(8,128)} %param.9) | copy-start | bytes 98308
  10.3 6.4 %copy-start.3 = (s32[16,512]{1,0:T(8,128)S(1)}, s32[16,512]{1,0:T(8,128)}, u32[]{:S(2)}) copy-start(s32[16,512]{1,0:T(8,128)} %param.8) | copy-start | bytes 98308
  10.3 6.4 %copy-start.4 = (s32[16,512]{1,0:T(8,128)S(1)}, s32[16,512]{1,0:T(8,128)}, u32[]{:S(2)}) copy-start(s32[16,512]{1,0:T(8,128)} %param.7) | copy-start | bytes 98308
  10.3 22.4 %all-to-all-start = ((bf16[8,2,64,512]{3,2,1,0:T(8,128)(2,1)}), bf16[8,2,64,512]{3,2,1,0:T(8,128)(2,1)S(1)}, u32[]{:S(2)}, u32[]{:S(2)}) async-start(bf16[8,2,64,512]{3,2,1,0:T(8,128)(2,1)} %get-tuple-element.4), calls=%async_computation | async-start | bytes 2097152 | tf_op jit(solution)/shard_map/all_to_all | solution.py:174
  16.7 6.1 %collective-permute-start.1 = (s32[3,8,512]{2,1,0:T(8,128)S(1)}, s32[3,8,512]{2,1,0:T(8,128)S(1)}, u32[]{:S(2)}, u32[]{:S(2)}) collective-permute-start(s32[3,8,512]{2,1,0:T(8,128)S(1)} %get-tuple-element.6), channel_id=1, source_target_pairs={{1,0},{2,1},{3,2},{4,3},{5,4},{6,5},{7,6},{8,7},{9,8},{10,9},{11,1... | collective-permute-start | bytes 147464 | tf_op jit(solution)/shard_map/ppermute | solution.py:125
  19.6 4.3 %collective-permute-start = (s32[3,8,512]{2,1,0:T(8,128)S(1)}, s32[3,8,512]{2,1,0:T(8,128)S(1)}, u32[]{:S(2)}, u32[]{:S(2)}) collective-permute-start(s32[3,8,512]{2,1,0:T(8,128)S(1)} %get-tuple-element.7), channel_id=1, source_target_pairs={{0,1},{1,2},{2,3},{3,4},{4,5},{5,6},{6,7},{7,8},{8,9},{9,10},{10,1... | collective-permute-start | bytes 147464 | tf_op jit(solution)/shard_map/ppermute | solution.py:125
where the time goes:
time: 35.4 us; the launch traced here: 35.1 us
  starting transfers between devices  12.3 us (35%)
  Pallas kernels  11.1 us (31%)
  waiting for transfers between devices  8.6 us (24%)
  local copies, waits for them, and re-layouts  2.28 us (6%)
  between operations  0.73 us (2%)
    all_to_all x1, waiting for transfers between devices, per_device(): lax.all_to_all(estimate, 'pair', split_axis=0, concat_axis=0, tiled=True)  7.57 us
    pallas_call x1, Pallas kernels, temporal_section(): pl.pallas_call(temporal_kernel, out_shape=(jax.ShapeDtypeStruct((peers, r...  7.43 us
    all_to_all x1, starting transfers between devices, per_device(): lax.all_to_all(estimate, 'pair', split_axis=0, concat_axis=0, tiled=True)  6.33 us
    ppermute x2, starting transfers between devices, shifted(): return lax.ppermute(value, axis, pairs)  5.97 us
    pallas_call x1, Pallas kernels, combine(): pl.pallas_call(combine_kernel, grid=(pairs // group,), out_shape=jax.Shap...  2.37 us
    unnamed x10, local copies, waits for them, and re-layouts  2.27 us
    pallas_call x1, Pallas kernels, deviation_section(): pl.pallas_call(deviation_kernel, out_shape=jax.ShapeDtypeStruct(cycles_do...  1.26 us
    ppermute x2, waiting for transfers between devices, shifted(): return lax.ppermute(value, axis, pairs)  1.03 us
  transfers between devices with their start and end apart: 3, of which 2 were waited for; matrix products, arithmetic and copies ran while one was open for 0% of the time, Pallas kernels for 4%

commit v1 on v0

--- a/solution.py
+++ b/solution.py
@@ -19,68 +19,117 @@
 
 HALO = 8
 LANES = 128
-VMEM_LIMIT = 40 * 2**20
+VMEM_LIMIT = 58 * 2**20
 
 
 def clip(value, bound):
     return jnp.minimum(jnp.maximum(value, -bound), bound)
 
 
-def temporal_kernel(wrapped_ref, projector_ref, estimate_ref, misfit_ref, phases_ref, multiplier_ref):
+def temporal_kernel(
+    wrapped_hbm,
+    projector_hbm,
+    estimate_hbm,
+    misfit_ref,
+    wrapped_ref,
+    projector_ref,
+    spread_ref,
+    phases_ref,
+    multiplier_ref,
+    blended_ref,
+    estimate_ref,
+    in_sems,
+    out_sems,
+):
     pairs = projector_ref.shape[0]
     per_pair = wrapped_ref.shape[0] // pairs
     peers, rows, group, _ = estimate_ref.shape
     pieces, _, width = multiplier_ref.shape
     wide = width // LANES
+    loads = in_sems.shape[0] - 1
+    load_rows = wrapped_ref.shape[0] // loads
+    load_pairs = pairs // loads
 
     def parts_of(piece):
-        return range(piece * wide, (piece + 1) * wide)
-
-    phases_ref[...] = wrapped_ref[...].astype(jnp.float32)
-    projector = projector_ref[...]
-
-    def phases_of(piece):
-        return jnp.concatenate([phases_ref[pl.ds(k, pairs, stride=per_pair), :] for k in parts_of(piece)], axis=1)
-
-    blended = [phases_of(piece).astype(jnp.bfloat16) for piece in range(pieces)]
+        return enumerate(range(piece * wide, (piece + 1) * wide))
+
+    copies = []
+    for load in range(loads):
+        part = pl.ds(load * load_rows, load_rows)
+        copies.append(pltpu.make_async_copy(wrapped_hbm.at[part], wrapped_ref.at[part], in_sems.at[load]))
+    copies.append(pltpu.make_async_copy(projector_hbm, projector_ref, in_sems.at[loads]))
+    for copy in copies:
+        copy.start()
+    for load in range(loads):
+        copies[load].wait()
+        first = load * load_rows
+        spread_ref[first : first + load_rows, :] = wrapped_ref[first : first + load_rows, :].astype(jnp.float32)
+        at_pairs = slice(load * load_pairs, (load + 1) * load_pairs)
+        for piece in range(pieces):
+            for at, k in parts_of(piece):
+                columns = slice(at * LANES, (at + 1) * LANES)
+                phases = spread_ref[pl.ds(first + k, load_pairs, stride=per_pair), :]
+                phases_ref[piece, at_pairs, columns] = phases
+                blended_ref[piece, at_pairs, columns] = phases.astype(jnp.bfloat16)
+    copies[loads].wait()
+
+    sent = []
     for iteration in range(TEMP_ITERS):
         for piece in range(pieces):
-            mapped = jnp.dot(projector, blended[piece], preferred_element_type=jnp.float32)
+            mapped = jnp.dot(projector_ref[...], blended_ref[piece], preferred_element_type=jnp.float32)
             carried = mapped if iteration == 0 else mapped + multiplier_ref[piece]
-            excess = carried - phases_of(piece)
+            excess = carried - phases_ref[piece]
             multiplier = clip(excess, SHRINK)
             if iteration < TEMP_ITERS - 1:
                 multiplier_ref[piece] = multiplier
-                blended[piece] = (carried - 2.0 * multiplier).astype(jnp.bfloat16)
+                blended_ref[piece] = (carried - 2.0 * multiplier).astype(jnp.bfloat16)
                 continue
             misfit = excess - multiplier
             estimate = mapped.astype(jnp.bfloat16)
-            for at, k in enumerate(parts_of(piece)):
+            for at, k in parts_of(piece):
                 columns = slice(at * LANES, (at + 1) * LANES)
-                misfit_ref[pl.ds(k, pairs, stride=per_pair), :] = misfit[:, columns]
                 tile, row = divmod(k, rows)
                 for peer in range(peers):
                     estimate_ref[peer, row, :, tile * LANES : (tile + 1) * LANES] = estimate[
                         peer * group : (peer + 1) * group, columns
                     ]
+            done = pl.ds(piece * width // rows, width // rows)
+            copy = pltpu.make_async_copy(
+                estimate_ref.at[:, :, :, done], estimate_hbm.at[:, :, :, done], out_sems.at[piece]
+            )
+            copy.start()
+            sent.append(copy)
+            for at, k in parts_of(piece):
+                misfit_ref[pl.ds(k, pairs, stride=per_pair), :] = misfit[:, at * LANES : (at + 1) * LANES]
+    for copy in sent:
+        copy.wait()
 
 
 def temporal_section(wrapped, projector, peers):
     pairs, rows, columns = wrapped.shape
     tiles = columns // LANES
     flat = wrapped.reshape(pairs, rows, tiles, LANES).transpose(0, 2, 1, 3).reshape(-1, LANES)
-    in_vmem = pl.BlockSpec(memory_space=pltpu.VMEM)
+    anywhere = pl.BlockSpec(memory_space=pl.ANY)
     width = 2 * LANES
     pieces = rows * columns // width
+    loads = 4
+    sent = (peers, rows, pairs // peers, columns)
     estimate, misfit = pl.pallas_call(
         temporal_kernel,
-        out_shape=(
-            jax.ShapeDtypeStruct((peers, rows, pairs // peers, columns), jnp.bfloat16),
-            jax.ShapeDtypeStruct(flat.shape, jnp.float32),
-        ),
-        in_specs=[in_vmem, in_vmem],
-        out_specs=(in_vmem, in_vmem),
-        scratch_shapes=[pltpu.VMEM(flat.shape, jnp.float32), pltpu.VMEM((pieces, pairs, width), jnp.float32)],
+        out_shape=(jax.ShapeDtypeStruct(sent, jnp.bfloat16), pltpu.VMEM(flat.shape, jnp.float32)),
+        in_specs=[anywhere, anywhere],
+        out_specs=(anywhere, pl.BlockSpec(memory_space=pltpu.VMEM)),
+        scratch_shapes=[
+            pltpu.VMEM(flat.shape, jnp.bfloat16),
+            pltpu.VMEM(projector.shape, jnp.bfloat16),
+            pltpu.VMEM(flat.shape, jnp.float32),
+            pltpu.VMEM((pieces, pairs, width), jnp.float32),
+            pltpu.VMEM((pieces, pairs, width), jnp.float32),
+            pltpu.VMEM((pieces, pairs, width), jnp.bfloat16),
+            pltpu.VMEM(sent, jnp.bfloat16),
+            pltpu.SemaphoreType.DMA((loads + 1,)),
+            pltpu.SemaphoreType.DMA((pieces,)),
+        ],
         compiler_params=pltpu.CompilerParams(vmem_limit_bytes=VMEM_LIMIT),
         cost_estimate=pl.CostEstimate(
             flops=2 * TEMP_ITERS * pairs * pairs * rows * columns, bytes_accessed=4 * 2**20, transcendentals=0
@@ -140,12 +189,23 @@
     )(above, own, below)
 
 
-def combine_kernel(order_ref, estimate_ref, deviation_ref, unwrapped_ref):
-    rows, group, columns = estimate_ref.shape
-    turned = jnp.dot(
-        order_ref[...], estimate_ref[...].reshape(rows * group, columns), preferred_element_type=jnp.float32
-    )
-    unwrapped_ref[...] = turned.reshape(group, rows, columns) + deviation_ref[...][None]
+def combine_kernel(order_ref, estimate_ref, deviation_ref, unwrapped_hbm, unwrapped_ref, sems):
+    rows, pairs, columns = estimate_ref.shape
+    group = order_ref.shape[0] // rows
+    sent = []
+    for at in range(pairs // group):
+        part = pl.ds(at * group, group)
+        turned = jnp.dot(
+            order_ref[...],
+            estimate_ref[:, part, :].reshape(rows * group, columns),
+            preferred_element_type=jnp.float32,
+        )
+        unwrapped_ref[part] = turned.reshape(group, rows, columns) + deviation_ref[...][None]
+        copy = pltpu.make_async_copy(unwrapped_ref.at[part], unwrapped_hbm.at[part], sems.at[at])
+        copy.start()
+        sent.append(copy)
+    for copy in sent:
+        copy.wait()
 
 
 def combine(estimate, deviation):
@@ -155,16 +215,13 @@
     place = jnp.arange(size)
     source = place % rows * group + place // rows
     order = (source[:, None] == place[None]).astype(jnp.bfloat16)
+    out = jax.ShapeDtypeStruct((pairs, rows, columns), jnp.float32)
     return pl.pallas_call(
         combine_kernel,
-        grid=(pairs // group,),
-        out_shape=jax.ShapeDtypeStruct((pairs, rows, columns), jnp.float32),
-        in_specs=[
-            pl.BlockSpec((size, size), lambda i: (0, 0)),
-            pl.BlockSpec((rows, group, columns), lambda i: (0, i, 0)),
-            pl.BlockSpec((rows, columns), lambda i: (0, 0)),
-        ],
-        out_specs=pl.BlockSpec((group, rows, columns), lambda i: (i, 0, 0)),
+        out_shape=out,
+        in_specs=[pl.BlockSpec(memory_space=pltpu.VMEM)] * 3,
+        out_specs=pl.BlockSpec(memory_space=pl.ANY),
+        scratch_shapes=[pltpu.VMEM(out.shape, out.dtype), pltpu.SemaphoreType.DMA((pairs // group,))],
         compiler_params=pltpu.CompilerParams(vmem_limit_bytes=16 * 2**20),
     )(order, estimate, deviation)
 

time: 35.4 us -> 31.2 us (0.88)
  Pallas kernels: 11.1 us -> 9.15 us
  waiting for transfers between devices: 8.6 us -> 7.28 us
  local copies, waits for them, and re-layouts: 2.28 us -> 1.35 us
    pallas_call x2, Pallas kernels: 9.8 us -> 7.88 us  [the longest x1 6.31 us: temporal_section(): pl.pallas_call(temporal_kernel, out_shape=(jax.ShapeDtypeStruct(sent, jnp...]
    ppermute x2, waiting for transfers between devices: 1.03 us -> 0.01 us  [shifted(): return lax.ppermute(value, axis, pairs)]
    unnamed x10 -> x7, local copies, waits for them, and re-layouts: 2.27 us -> 1.34 us
  transfers between devices with their start and end apart: 3 -> 3, of which waited for: 2 -> 1; matrix products, arithmetic and copies ran while one was open for 0% -> 5% of each run, Pallas kernels for 4% -> 4%
where the time goes in v1:
time: 31.2 us; the launch traced here: 30.9 us
  starting transfers between devices  12.3 us (39%)
  Pallas kernels  9.15 us (29%)
  waiting for transfers between devices  7.28 us (23%)
  local copies, waits for them, and re-layouts  1.35 us (4%)
  between operations  0.74 us (2%)
    all_to_all x1, waiting for transfers between devices, per_device(): lax.all_to_all(estimate, 'pair', split_axis=0, concat_axis=0, tiled=True)  7.27 us
    all_to_all x1, starting transfers between devices, per_device(): lax.all_to_all(estimate, 'pair', split_axis=0, concat_axis=0, tiled=True)  6.34 us
    pallas_call x1, Pallas kernels, temporal_section(): pl.pallas_call(temporal_kernel, out_shape=(jax.ShapeDtypeStruct(sent, jnp...  6.31 us
    ppermute x2, starting transfers between devices, shifted(): return lax.ppermute(value, axis, pairs)  5.97 us
    pallas_call x1, Pallas kernels, combine(): pl.pallas_call(combine_kernel, out_shape=out, in_specs=[pl.BlockSpec(memo...  1.58 us
    unnamed x7, local copies, waits for them, and re-layouts  1.34 us
    pallas_call x1, Pallas kernels, deviation_section(): pl.pallas_call(deviation_kernel, out_shape=jax.ShapeDtypeStruct(cycles_do...  1.26 us
  transfers between devices with their start and end apart: 3, of which 1 were waited for; matrix products, arithmetic and copies ran while one was open for 5% of the time, Pallas kernels for 4%

profile of v1, /device:TPU:1, one launch (start us, length us, event | category | flops | bytes accessed | tf_op | source)
XLA Modules:
  0.0 30.9 jit_solution(953661793375431065)
XLA Ops:
  0.6 6.3 %shard_map.68 = (bf16[8,2,64,512]{3,2,1,0:T(8,128)(2,1)}, f32[4096,128]{1,0:T(8,128)S(1)}) custom-call(bf16[4096,128]{1,0:T(8,128)(2,1)} %bitcast.19, bf16[512,512]{1,0:T(8,128)(2,1)} %projector_hbm.1), custom_call_target="tpu_custom_call" | custom-call | flops 3221225472 | bytes 4194304 | tf_op jit(solution)/shard_map/pallas_call | solution.py:117
  6.9 0.0 copy-start
  7.0 0.0 copy-start.1
  7.0 0.0 copy-start.2
  7.0 6.3 %all-to-all-start = ((bf16[8,2,64,512]{3,2,1,0:T(8,128)(2,1)}), bf16[8,2,64,512]{3,2,1,0:T(8,128)(2,1)S(1)}, u32[]{:S(2)}, u32[]{:S(2)}) async-start(bf16[8,2,64,512]{3,2,1,0:T(8,128)(2,1)} %get-tuple-element.4), calls=%async_computation | async-start | bytes 2097152 | tf_op jit(solution)/shard_map/all_to_all | solution.py:231
  13.3 0.0 copy-done
  13.3 0.0 copy-done.1
  13.4 0.0 copy-done.2
  13.4 2.9 %collective-permute-start.1 = (s32[3,8,512]{2,1,0:T(8,128)S(1)}, s32[3,8,512]{2,1,0:T(8,128)S(1)}, u32[]{:S(2)}, u32[]{:S(2)}) collective-permute-start(s32[3,8,512]{2,1,0:T(8,128)S(1)} %get-tuple-element.6), channel_id=1, source_target_pairs={{1,0},{2,1},{3,2},{4,3},{5,4},{6,5},{7,6},{8,7},{9,8},{10,9},{11,1... | collective-permute-start | bytes 147464 | tf_op jit(solution)/shard_map/ppermute | solution.py:174
  16.3 3.1 %collective-permute-start = (s32[3,8,512]{2,1,0:T(8,128)S(1)}, s32[3,8,512]{2,1,0:T(8,128)S(1)}, u32[]{:S(2)}, u32[]{:S(2)}) collective-permute-start(s32[3,8,512]{2,1,0:T(8,128)S(1)} %get-tuple-element.7), channel_id=1, source_target_pairs={{0,1},{1,2},{2,3},{3,4},{4,5},{5,6},{6,7},{7,8},{8,9},{9,10},{10,1... | collective-permute-start | bytes 147464 | tf_op jit(solution)/shard_map/ppermute | solution.py:174
  19.4 0.1 fusion.order_ref
  19.5 1.3 %copy.9 = f32[512,2,512]{2,1,0:T(2,128)} copy(f32[512,2,512]{2,1,0:T(2,128)S(1)} %bitcast.15) | data formatting | bytes 4194304
  20.8 0.0 collective-permute-done.1.below_ref
  20.8 0.0 collective-permute-done.above_ref
  20.8 1.3 %shard_map.69.deviation_ref = f32[16,512]{1,0:T(8,128)S(1)} custom-call(s32[3,8,512]{2,1,0:T(8,128)S(1)} %collective-permute-done.above_ref, s32[3,16,512]{2,1,0:T(8,128)S(1)} %pad_add_fusion.own_ref, s32[3,8,512]{2,1,0:T(8,128)S(1)} %collective-permute-done.1.below_ref), custom_call_target="tpu_custom_call" | custom-call | flops 4194304 | bytes 262144 | tf_op jit(solution)/shard_map/pallas_call | solution.py:182
  22.1 7.3 %all-to-all-done = bf16[8,2,64,512]{3,2,1,0:T(8,128)(2,1)S(1)} async-done(((bf16[8,2,64,512]{3,2,1,0:T(8,128)(2,1)}), bf16[8,2,64,512]{3,2,1,0:T(8,128)(2,1)S(1)}, u32[]{:S(2)}, u32[]{:S(2)}) %all-to-all-start) | async-done | bytes 1048608 | tf_op jit(solution)/shard_map/all_to_all | solution.py:231
  29.4 1.6 %shard_map.70 = f32[64,16,512]{2,1,0:T(8,128)} custom-call(bf16[256,256]{1,0:T(8,128)(2,1)S(1)} %fusion.order_ref, bf16[16,64,512]{2,1,0:T(8,128)(2,1)S(1)} %bitcast.16, f32[16,512]{1,0:T(8,128)S(1)} %shard_map.69.deviation_ref), custom_call_target="tpu_custom_call" | custom-call | tf_op jit(solution)/shard_map/pallas_call | solution.py:219
  (4 shorter events, 0.0 us)
Async XLA Ops:
  6.9 6.4 %copy-start = (s32[16,512]{1,0:T(8,128)S(1)}, s32[16,512]{1,0:T(8,128)}, u32[]{:S(2)}) copy-start(s32[16,512]{1,0:T(8,128)} %param.9) | copy-start | bytes 98308
  7.0 6.4 %copy-start.1 = (s32[16,512]{1,0:T(8,128)S(1)}, s32[16,512]{1,0:T(8,128)}, u32[]{:S(2)}) copy-start(s32[16,512]{1,0:T(8,128)} %param.8) | copy-start | bytes 98308
  7.0 6.4 %copy-start.2 = (s32[16,512]{1,0:T(8,128)S(1)}, s32[16,512]{1,0:T(8,128)}, u32[]{:S(2)}) copy-start(s32[16,512]{1,0:T(8,128)} %param.7) | copy-start | bytes 98308
  7.0 22.4 %all-to-all-start = ((bf16[8,2,64,512]{3,2,1,0:T(8,128)(2,1)}), bf16[8,2,64,512]{3,2,1,0:T(8,128)(2,1)S(1)}, u32[]{:S(2)}, u32[]{:S(2)}) async-start(bf16[8,2,64,512]{3,2,1,0:T(8,128)(2,1)} %get-tuple-element.4), calls=%async_computation | async-start | bytes 2097152 | tf_op jit(solution)/shard_map/all_to_all | solution.py:231
  13.4 7.4 %collective-permute-start.1 = (s32[3,8,512]{2,1,0:T(8,128)S(1)}, s32[3,8,512]{2,1,0:T(8,128)S(1)}, u32[]{:S(2)}, u32[]{:S(2)}) collective-permute-start(s32[3,8,512]{2,1,0:T(8,128)S(1)} %get-tuple-element.6), channel_id=1, source_target_pairs={{1,0},{2,1},{3,2},{4,3},{5,4},{6,5},{7,6},{8,7},{9,8},{10,9},{11,1... | collective-permute-start | bytes 147464 | tf_op jit(solution)/shard_map/ppermute | solution.py:174
  16.3 4.6 %collective-permute-start = (s32[3,8,512]{2,1,0:T(8,128)S(1)}, s32[3,8,512]{2,1,0:T(8,128)S(1)}, u32[]{:S(2)}, u32[]{:S(2)}) collective-permute-start(s32[3,8,512]{2,1,0:T(8,128)S(1)} %get-tuple-element.7), channel_id=1, source_target_pairs={{0,1},{1,2},{2,3},{3,4},{4,5},{5,6},{6,7},{7,8},{8,9},{9,10},{10,1... | collective-permute-start | bytes 147464 | tf_op jit(solution)/shard_map/ppermute | solution.py:174

commit v2 on v1

--- a/solution.py
+++ b/solution.py
@@ -73,34 +73,40 @@
                 blended_ref[piece, at_pairs, columns] = phases.astype(jnp.bfloat16)
     copies[loads].wait()
 
+    half = pairs // 2
     sent = []
     for iteration in range(TEMP_ITERS):
         for piece in range(pieces):
-            mapped = jnp.dot(projector_ref[...], blended_ref[piece], preferred_element_type=jnp.float32)
-            carried = mapped if iteration == 0 else mapped + multiplier_ref[piece]
-            excess = carried - phases_ref[piece]
-            multiplier = clip(excess, SHRINK)
-            if iteration < TEMP_ITERS - 1:
-                multiplier_ref[piece] = multiplier
-                blended_ref[piece] = (carried - 2.0 * multiplier).astype(jnp.bfloat16)
-                continue
-            misfit = excess - multiplier
-            estimate = mapped.astype(jnp.bfloat16)
-            for at, k in parts_of(piece):
-                columns = slice(at * LANES, (at + 1) * LANES)
-                tile, row = divmod(k, rows)
-                for peer in range(peers):
-                    estimate_ref[peer, row, :, tile * LANES : (tile + 1) * LANES] = estimate[
-                        peer * group : (peer + 1) * group, columns
-                    ]
-            done = pl.ds(piece * width // rows, width // rows)
-            copy = pltpu.make_async_copy(
-                estimate_ref.at[:, :, :, done], estimate_hbm.at[:, :, :, done], out_sems.at[piece]
-            )
-            copy.start()
-            sent.append(copy)
-            for at, k in parts_of(piece):
-                misfit_ref[pl.ds(k, pairs, stride=per_pair), :] = misfit[:, at * LANES : (at + 1) * LANES]
+            blended, following = blended_ref[piece], []
+            for begin in (0, half):
+                part = slice(begin, begin + half)
+                mapped = jnp.dot(projector_ref[part, :], blended, preferred_element_type=jnp.float32)
+                carried = mapped if iteration == 0 else mapped + multiplier_ref[piece, part]
+                excess = carried - phases_ref[piece, part]
+                multiplier = clip(excess, SHRINK)
+                if iteration < TEMP_ITERS - 1:
+                    multiplier_ref[piece, part] = multiplier
+                    following.append((carried - 2.0 * multiplier).astype(jnp.bfloat16))
+                    continue
+                misfit = excess - multiplier
+                estimate = mapped.astype(jnp.bfloat16)
+                for at, k in parts_of(piece):
+                    columns = slice(at * LANES, (at + 1) * LANES)
+                    tile, row = divmod(k, rows)
+                    for block in range(half // group):
+                        estimate_ref[begin // group + block, row, :, tile * LANES : (tile + 1) * LANES] = estimate[
+                            block * group : (block + 1) * group, columns
+                        ]
+                    misfit_ref[pl.ds(begin * per_pair + k, half, stride=per_pair), :] = misfit[:, columns]
+            for begin, value in zip((0, half), following):
+                blended_ref[piece, begin : begin + half] = value
+            if iteration == TEMP_ITERS - 1:
+                done = pl.ds(piece * width // rows, width // rows)
+                copy = pltpu.make_async_copy(
+                    estimate_ref.at[:, :, :, done], estimate_hbm.at[:, :, :, done], out_sems.at[piece]
+                )
+                copy.start()
+                sent.append(copy)
     for copy in sent:
         copy.wait()
 
@@ -176,8 +182,15 @@
 
 def deviation_section(cycles_down, cycles_across, weight_class):
     own = jnp.stack([cycles_down, cycles_across, weight_class + 1])
-    above = shifted(own[:, -HALO:], "tile", 1)
-    below = shifted(own[:, :HALO], "tile", -1)
+    tiles = lax.axis_size("tile")
+    tile = lax.axis_index("tile")
+    even = tile % 2 == 0
+    top, bottom = own[:, :HALO], own[:, -HALO:]
+    inner = lax.ppermute(jnp.where(even, bottom, top), "tile", [(i, i ^ 1) for i in range(tiles)])
+    outer = lax.ppermute(
+        jnp.where(even, top, bottom), "tile", [(i, i - 1 if i % 2 == 0 else i + 1) for i in range(1, tiles - 1)]
+    )
+    above, below = jnp.where(even, outer, inner), jnp.where(even, inner, outer)
     in_vmem = pl.BlockSpec(memory_space=pltpu.VMEM)
     return pl.pallas_call(
         deviation_kernel,

time: 31.2 us -> 30.8 us (0.987)
  starting transfers between devices: 12.3 us -> 10.5 us
  waiting for transfers between devices: 7.28 us -> 8.85 us
    ppermute x2, starting transfers between devices: 5.97 us -> 4.14 us  [the longest x1 3.1 us: deviation_section(): lax.ppermute(jnp.where(even, top, bottom), 'tile', [(i, i - 1 if i % 2 ==...]
    ppermute x2, waiting for transfers between devices: 0.01 us -> 1.14 us  [the longest x1 1.14 us: deviation_section(): lax.ppermute(jnp.where(even, top, bottom), 'tile', [(i, i - 1 if i % 2 ==...]
    all_to_all x1, waiting for transfers between devices: 7.27 us -> 7.71 us  [per_device(): lax.all_to_all(estimate, 'pair', split_axis=0, concat_axis=0, tiled=True)]
  transfers between devices with their start and end apart: 3 -> 3, of which waited for: 1 -> 2; matrix products, arithmetic and copies ran while one was open for 5% -> 5% of each run, Pallas kernels for 4% -> 4%
where the time goes in v2:
time: 30.8 us; the launch traced here: 30.5 us
  starting transfers between devices  10.5 us (34%)
  Pallas kernels  8.93 us (29%)
  waiting for transfers between devices  8.85 us (29%)
  local copies, waits for them, and re-layouts  1.34 us (4%)
  between operations  0.75 us (2%)
    all_to_all x1, waiting for transfers between devices, per_device(): lax.all_to_all(estimate, 'pair', split_axis=0, concat_axis=0, tiled=True)  7.71 us
    all_to_all x1, starting transfers between devices, per_device(): lax.all_to_all(estimate, 'pair', split_axis=0, concat_axis=0, tiled=True)  6.35 us
    pallas_call x1, Pallas kernels, temporal_section(): pl.pallas_call(temporal_kernel, out_shape=(jax.ShapeDtypeStruct(sent, jnp...  6.09 us
    ppermute x1, starting transfers between devices, deviation_section(): lax.ppermute(jnp.where(even, top, bottom), 'tile', [(i, i - 1 if i % 2 ==...  3.1 us
    pallas_call x1, Pallas kernels, combine(): pl.pallas_call(combine_kernel, out_shape=out, in_specs=[pl.BlockSpec(memo...  1.58 us
    unnamed x7, local copies, waits for them, and re-layouts  1.34 us
    pallas_call x1, Pallas kernels, deviation_section(): pl.pallas_call(deviation_kernel, out_shape=jax.ShapeDtypeStruct(cycles_do...  1.26 us
    ppermute x1, waiting for transfers between devices, deviation_section(): lax.ppermute(jnp.where(even, top, bottom), 'tile', [(i, i - 1 if i % 2 ==...  1.14 us
  transfers between devices with their start and end apart: 3, of which 2 were waited for; matrix products, arithmetic and copies ran while one was open for 5% of the time, Pallas kernels for 4%

profile of v2, /device:TPU:1, one launch (start us, length us, event | category | flops | bytes accessed | tf_op | source)
XLA Modules:
  0.0 30.5 jit_solution(10322376282161755966)
XLA Ops:
  0.6 6.1 %shard_map.68 = (bf16[8,2,64,512]{3,2,1,0:T(8,128)(2,1)}, f32[4096,128]{1,0:T(8,128)S(1)}) custom-call(bf16[4096,128]{1,0:T(8,128)(2,1)} %bitcast.19, bf16[512,512]{1,0:T(8,128)(2,1)} %projector_hbm.1), custom_call_target="tpu_custom_call" | custom-call | flops 3221225472 | bytes 4194304 | tf_op jit(solution)/shard_map/pallas_call | solution.py:123
  6.7 0.0 copy-start
  6.7 0.0 copy-start.1
  6.8 0.0 copy-start.2
  6.8 6.3 %all-to-all-start = ((bf16[8,2,64,512]{3,2,1,0:T(8,128)(2,1)}), bf16[8,2,64,512]{3,2,1,0:T(8,128)(2,1)S(1)}, u32[]{:S(2)}, u32[]{:S(2)}) async-start(bf16[8,2,64,512]{3,2,1,0:T(8,128)(2,1)} %get-tuple-element.4), calls=%async_computation | async-start | bytes 2097152 | tf_op jit(solution)/shard_map/all_to_all | solution.py:244
  13.1 0.0 copy-done
  13.1 0.0 copy-done.1
  13.2 0.0 copy-done.2
  13.2 1.0 %collective-permute-start.1 = (s32[3,8,512]{2,1,0:T(8,128)S(1)}, s32[3,8,512]{2,1,0:T(8,128)S(1)}, u32[]{:S(2)}, u32[]{:S(2)}) collective-permute-start(s32[3,8,512]{2,1,0:T(8,128)S(1)} %get-tuple-element.8), channel_id=1, source_target_pairs={{0,1},{1,0},{2,3},{3,2},{4,5},{5,4},{6,7},{7,6},{8,9},{9,8},{10,11... | collective-permute-start | bytes 147464 | tf_op jit(solution)/shard_map/ppermute | solution.py:189
  14.2 3.1 %collective-permute-start = (s32[3,8,512]{2,1,0:T(8,128)S(1)}, s32[3,8,512]{2,1,0:T(8,128)S(1)}, u32[]{:S(2)}, u32[]{:S(2)}) collective-permute-start(s32[3,8,512]{2,1,0:T(8,128)S(1)} %get-tuple-element.9), channel_id=1, source_target_pairs={{1,2},{2,1},{3,4},{4,3},{5,6},{6,5},{7,8},{8,7},{9,10},{10,9},{11,... | collective-permute-start | bytes 147464 | tf_op jit(solution)/shard_map/ppermute | solution.py:190
  17.4 0.1 fusion.order_ref
  17.5 1.3 %copy.9 = f32[512,2,512]{2,1,0:T(2,128)} copy(f32[512,2,512]{2,1,0:T(2,128)S(1)} %bitcast.15) | data formatting | bytes 4194304
  18.8 0.0 collective-permute-done.1
  18.8 1.1 %collective-permute-done = s32[3,8,512]{2,1,0:T(8,128)S(1)} collective-permute-done((s32[3,8,512]{2,1,0:T(8,128)S(1)}, s32[3,8,512]{2,1,0:T(8,128)S(1)}, u32[]{:S(2)}, u32[]{:S(2)}) %collective-permute-start) | collective-permute-done | bytes 49184 | tf_op jit(solution)/shard_map/ppermute | solution.py:190
  19.9 1.3 %shard_map.69.deviation_ref = f32[16,512]{1,0:T(8,128)S(1)} custom-call(s32[3,8,512]{2,1,0:T(8,128)S(1)} %get-tuple-element.7.above_ref, s32[3,16,512]{2,1,0:T(8,128)S(1)} %pad_add_fusion.own_ref, s32[3,8,512]{2,1,0:T(8,128)S(1)} %get-tuple-element.6.below_ref), custom_call_target="tpu_custom_call" | custom-call | flops 4194304 | bytes 262144 | tf_op jit(solution)/shard_map/pallas_call | solution.py:195
  21.2 7.7 %all-to-all-done = bf16[8,2,64,512]{3,2,1,0:T(8,128)(2,1)S(1)} async-done(((bf16[8,2,64,512]{3,2,1,0:T(8,128)(2,1)}), bf16[8,2,64,512]{3,2,1,0:T(8,128)(2,1)S(1)}, u32[]{:S(2)}, u32[]{:S(2)}) %all-to-all-start) | async-done | bytes 1048608 | tf_op jit(solution)/shard_map/all_to_all | solution.py:244
  28.9 1.6 %shard_map.70 = f32[64,16,512]{2,1,0:T(8,128)} custom-call(bf16[256,256]{1,0:T(8,128)(2,1)S(1)} %fusion.order_ref, bf16[16,64,512]{2,1,0:T(8,128)(2,1)S(1)} %bitcast.16, f32[16,512]{1,0:T(8,128)S(1)} %shard_map.69.deviation_ref), custom_call_target="tpu_custom_call" | custom-call | tf_op jit(solution)/shard_map/pallas_call | solution.py:232
  (5 shorter events, 0.0 us)
Async XLA Ops:
  6.7 6.4 %copy-start = (s32[16,512]{1,0:T(8,128)S(1)}, s32[16,512]{1,0:T(8,128)}, u32[]{:S(2)}) copy-start(s32[16,512]{1,0:T(8,128)} %param.9) | copy-start | bytes 98308
  6.7 6.4 %copy-start.1 = (s32[16,512]{1,0:T(8,128)S(1)}, s32[16,512]{1,0:T(8,128)}, u32[]{:S(2)}) copy-start(s32[16,512]{1,0:T(8,128)} %param.8) | copy-start | bytes 98308
  6.8 6.4 %copy-start.2 = (s32[16,512]{1,0:T(8,128)S(1)}, s32[16,512]{1,0:T(8,128)}, u32[]{:S(2)}) copy-start(s32[16,512]{1,0:T(8,128)} %param.7) | copy-start | bytes 98308
  6.8 22.2 %all-to-all-start = ((bf16[8,2,64,512]{3,2,1,0:T(8,128)(2,1)}), bf16[8,2,64,512]{3,2,1,0:T(8,128)(2,1)S(1)}, u32[]{:S(2)}, u32[]{:S(2)}) async-start(bf16[8,2,64,512]{3,2,1,0:T(8,128)(2,1)} %get-tuple-element.4), calls=%async_computation | async-start | bytes 2097152 | tf_op jit(solution)/shard_map/all_to_all | solution.py:244
  13.2 5.6 %collective-permute-start.1 = (s32[3,8,512]{2,1,0:T(8,128)S(1)}, s32[3,8,512]{2,1,0:T(8,128)S(1)}, u32[]{:S(2)}, u32[]{:S(2)}) collective-permute-start(s32[3,8,512]{2,1,0:T(8,128)S(1)} %get-tuple-element.8), channel_id=1, source_target_pairs={{0,1},{1,0},{2,3},{3,2},{4,5},{5,4},{6,7},{7,6},{8,9},{9,8},{10,11... | collective-permute-start | bytes 147464 | tf_op jit(solution)/shard_map/ppermute | solution.py:189
  14.2 5.7 %collective-permute-start = (s32[3,8,512]{2,1,0:T(8,128)S(1)}, s32[3,8,512]{2,1,0:T(8,128)S(1)}, u32[]{:S(2)}, u32[]{:S(2)}) collective-permute-start(s32[3,8,512]{2,1,0:T(8,128)S(1)} %get-tuple-element.9), channel_id=1, source_target_pairs={{1,2},{2,1},{3,4},{4,3},{5,6},{6,5},{7,8},{8,7},{9,10},{10,9},{11,... | collective-permute-start | bytes 147464 | tf_op jit(solution)/shard_map/ppermute | solution.py:190

commit v3 on v2

--- a/solution.py
+++ b/solution.py
@@ -30,7 +30,7 @@
     wrapped_hbm,
     projector_hbm,
     estimate_hbm,
-    misfit_ref,
+    excess_ref,
     wrapped_ref,
     projector_ref,
     spread_ref,
@@ -88,7 +88,7 @@
                     multiplier_ref[piece, part] = multiplier
                     following.append((carried - 2.0 * multiplier).astype(jnp.bfloat16))
                     continue
-                misfit = excess - multiplier
+                excess_ref[piece, part] = excess
                 estimate = mapped.astype(jnp.bfloat16)
                 for at, k in parts_of(piece):
                     columns = slice(at * LANES, (at + 1) * LANES)
@@ -97,7 +97,6 @@
                         estimate_ref[begin // group + block, row, :, tile * LANES : (tile + 1) * LANES] = estimate[
                             block * group : (block + 1) * group, columns
                         ]
-                    misfit_ref[pl.ds(begin * per_pair + k, half, stride=per_pair), :] = misfit[:, columns]
             for begin, value in zip((0, half), following):
                 blended_ref[piece, begin : begin + half] = value
             if iteration == TEMP_ITERS - 1:
@@ -111,6 +110,20 @@
         copy.wait()
 
 
+def misfit_kernel(excess_ref, misfit_hbm, misfit_ref, sem):
+    pieces, pairs, width = excess_ref.shape
+    wide = width // LANES
+    for piece in range(pieces):
+        excess = excess_ref[piece]
+        misfit = excess - clip(excess, SHRINK)
+        for at in range(wide):
+            rows = pl.ds(piece * wide + at, pairs, stride=pieces * wide)
+            misfit_ref[rows, :] = misfit[:, at * LANES : (at + 1) * LANES]
+    copy = pltpu.make_async_copy(misfit_ref, misfit_hbm, sem)
+    copy.start()
+    copy.wait()
+
+
 def temporal_section(wrapped, projector, peers):
     pairs, rows, columns = wrapped.shape
     tiles = columns // LANES
@@ -120,9 +133,9 @@
     pieces = rows * columns // width
     loads = 4
     sent = (peers, rows, pairs // peers, columns)
-    estimate, misfit = pl.pallas_call(
+    estimate, excess = pl.pallas_call(
         temporal_kernel,
-        out_shape=(jax.ShapeDtypeStruct(sent, jnp.bfloat16), pltpu.VMEM(flat.shape, jnp.float32)),
+        out_shape=(jax.ShapeDtypeStruct(sent, jnp.bfloat16), pltpu.VMEM((pieces, pairs, width), jnp.float32)),
         in_specs=[anywhere, anywhere],
         out_specs=(anywhere, pl.BlockSpec(memory_space=pltpu.VMEM)),
         scratch_shapes=[
@@ -141,6 +154,15 @@
             flops=2 * TEMP_ITERS * pairs * pairs * rows * columns, bytes_accessed=4 * 2**20, transcendentals=0
         ),
     )(flat, projector)
+    misfit = pl.pallas_call(
+        misfit_kernel,
+        out_shape=jax.ShapeDtypeStruct(flat.shape, jnp.float32),
+        in_specs=[pl.BlockSpec(memory_space=pltpu.VMEM)],
+        out_specs=anywhere,
+        scratch_shapes=[pltpu.VMEM(flat.shape, jnp.float32), pltpu.SemaphoreType.DMA],
+        compiler_params=pltpu.CompilerParams(vmem_limit_bytes=16 * 2**20),
+        cost_estimate=pl.CostEstimate(flops=2**21, bytes_accessed=2**22, transcendentals=0),
+    )(excess)
     misfit = misfit.reshape(pairs, tiles, rows, LANES).transpose(0, 2, 1, 3).reshape(pairs, rows, columns)
     return estimate, misfit
 

time: 30.8 us -> 30.6 us (level)
  Pallas kernels: 8.93 us -> 10.7 us
  local copies, waits for them, and re-layouts: 1.34 us -> 0.02 us
  waiting for transfers between devices: 8.85 us -> 8.24 us
    pallas_call x0 -> x1, Pallas kernels: none -> 1.92 us  [temporal_section(): pl.pallas_call(misfit_kernel, out_shape=jax.ShapeDtypeStruct(flat.shape,...]
    unnamed x7 -> x6, local copies, waits for them, and re-layouts: 1.34 us -> 0.02 us
    ppermute x1, waiting for transfers between devices: 1.14 us -> 0.52 us  [deviation_section(): lax.ppermute(jnp.where(even, top, bottom), 'tile', [(i, i - 1 if i % 2 ==...]
  transfers between devices with their start and end apart: 3 -> 3, of which waited for: 2 -> 2; matrix products, arithmetic and copies ran while one was open for 5% -> 0% of each run, Pallas kernels for 4% -> 11%
where the time goes in v3:
time: 30.6 us; the launch traced here: 30.3 us
  Pallas kernels  10.7 us (35%)
  starting transfers between devices  10.5 us (34%)
  waiting for transfers between devices  8.24 us (27%)
  between operations  0.77 us (3%)
    all_to_all x1, waiting for transfers between devices, per_device(): lax.all_to_all(estimate, 'pair', split_axis=0, concat_axis=0, tiled=True)  7.71 us
    all_to_all x1, starting transfers between devices, per_device(): lax.all_to_all(estimate, 'pair', split_axis=0, concat_axis=0, tiled=True)  6.35 us
    pallas_call x1, Pallas kernels, temporal_section(): pl.pallas_call(temporal_kernel, out_shape=(jax.ShapeDtypeStruct(sent, jnp...  5.92 us
    ppermute x1, starting transfers between devices, deviation_section(): lax.ppermute(jnp.where(even, top, bottom), 'tile', [(i, i - 1 if i % 2 ==...  3.1 us
    pallas_call x1, Pallas kernels, temporal_section(): pl.pallas_call(misfit_kernel, out_shape=jax.ShapeDtypeStruct(flat.shape,...  1.92 us
    pallas_call x1, Pallas kernels, combine(): pl.pallas_call(combine_kernel, out_shape=out, in_specs=[pl.BlockSpec(memo...  1.58 us
    pallas_call x1, Pallas kernels, deviation_section(): pl.pallas_call(deviation_kernel, out_shape=jax.ShapeDtypeStruct(cycles_do...  1.26 us
    ppermute x1, starting transfers between devices, deviation_section(): lax.ppermute(jnp.where(even, bottom, top), 'tile', [(i, i ^ 1) for i in r...  1.04 us
  transfers between devices with their start and end apart: 3, of which 2 were waited for; matrix products, arithmetic and copies ran while one was open for 0% of the time, Pallas kernels for 11%

profile of v3, /device:TPU:1, one launch (start us, length us, event | category | flops | bytes accessed | tf_op | source)
XLA Modules:
  0.0 30.3 jit_solution(2846541335466358124)
XLA Ops:
  0.6 5.9 %shard_map.68 = (bf16[8,2,64,512]{3,2,1,0:T(8,128)(2,1)}, f32[4,512,256]{2,1,0:T(8,128)S(1)}) custom-call(bf16[4096,128]{1,0:T(8,128)(2,1)} %bitcast.19, bf16[512,512]{1,0:T(8,128)(2,1)} %projector_hbm.1), custom_call_target="tpu_custom_call" | custom-call | flops 3221225472 | bytes 4194304 | tf_op jit(solution)/shard_map/pallas_call | solution.py:136
  6.6 0.0 copy-start
  6.6 0.0 copy-start.1
  6.6 0.0 copy-start.2
  6.6 6.3 %all-to-all-start = ((bf16[8,2,64,512]{3,2,1,0:T(8,128)(2,1)}), bf16[8,2,64,512]{3,2,1,0:T(8,128)(2,1)S(1)}, u32[]{:S(2)}, u32[]{:S(2)}) async-start(bf16[8,2,64,512]{3,2,1,0:T(8,128)(2,1)} %get-tuple-element.4), calls=%async_computation | async-start | bytes 2097152 | tf_op jit(solution)/shard_map/all_to_all | solution.py:266
  12.9 0.0 copy-done
  13.0 0.0 copy-done.1
  13.0 0.0 copy-done.2
  13.0 1.0 %collective-permute-start.1 = (s32[3,8,512]{2,1,0:T(8,128)S(1)}, s32[3,8,512]{2,1,0:T(8,128)S(1)}, u32[]{:S(2)}, u32[]{:S(2)}) collective-permute-start(s32[3,8,512]{2,1,0:T(8,128)S(1)} %get-tuple-element.8), channel_id=1, source_target_pairs={{0,1},{1,0},{2,3},{3,2},{4,5},{5,4},{6,7},{7,6},{8,9},{9,8},{10,11... | collective-permute-start | bytes 147464 | tf_op jit(solution)/shard_map/ppermute | solution.py:211
  14.1 3.1 %collective-permute-start = (s32[3,8,512]{2,1,0:T(8,128)S(1)}, s32[3,8,512]{2,1,0:T(8,128)S(1)}, u32[]{:S(2)}, u32[]{:S(2)}) collective-permute-start(s32[3,8,512]{2,1,0:T(8,128)S(1)} %get-tuple-element.9), channel_id=1, source_target_pairs={{1,2},{2,1},{3,4},{4,3},{5,6},{6,5},{7,8},{8,7},{9,10},{10,9},{11,... | collective-permute-start | bytes 147464 | tf_op jit(solution)/shard_map/ppermute | solution.py:212
  17.2 0.1 fusion.order_ref
  17.3 1.9 %shard_map.71 = f32[4096,128]{1,0:T(8,128)} custom-call(f32[4,512,256]{2,1,0:T(8,128)S(1)} %get-tuple-element.5.excess_ref), custom_call_target="tpu_custom_call" | custom-call | flops 2097152 | bytes 4194304 | tf_op jit(solution)/shard_map/pallas_call | solution.py:157
  19.2 0.0 collective-permute-done.1
  19.2 0.5 %collective-permute-done = s32[3,8,512]{2,1,0:T(8,128)S(1)} collective-permute-done((s32[3,8,512]{2,1,0:T(8,128)S(1)}, s32[3,8,512]{2,1,0:T(8,128)S(1)}, u32[]{:S(2)}, u32[]{:S(2)}) %collective-permute-start) | collective-permute-done | bytes 49184 | tf_op jit(solution)/shard_map/ppermute | solution.py:212
  19.8 1.3 %shard_map.69.deviation_ref = f32[16,512]{1,0:T(8,128)S(1)} custom-call(s32[3,8,512]{2,1,0:T(8,128)S(1)} %get-tuple-element.7.above_ref, s32[3,16,512]{2,1,0:T(8,128)S(1)} %pad_add_fusion.own_ref, s32[3,8,512]{2,1,0:T(8,128)S(1)} %get-tuple-element.6.below_ref), custom_call_target="tpu_custom_call" | custom-call | flops 4194304 | bytes 262144 | tf_op jit(solution)/shard_map/pallas_call | solution.py:217
  21.0 7.7 %all-to-all-done = bf16[8,2,64,512]{3,2,1,0:T(8,128)(2,1)S(1)} async-done(((bf16[8,2,64,512]{3,2,1,0:T(8,128)(2,1)}), bf16[8,2,64,512]{3,2,1,0:T(8,128)(2,1)S(1)}, u32[]{:S(2)}, u32[]{:S(2)}) %all-to-all-start) | async-done | bytes 1048608 | tf_op jit(solution)/shard_map/all_to_all | solution.py:266
  28.7 1.6 %shard_map.70 = f32[64,16,512]{2,1,0:T(8,128)} custom-call(bf16[256,256]{1,0:T(8,128)(2,1)S(1)} %fusion.order_ref, bf16[16,64,512]{2,1,0:T(8,128)(2,1)S(1)} %bitcast.15, f32[16,512]{1,0:T(8,128)S(1)} %shard_map.69.deviation_ref), custom_call_target="tpu_custom_call" | custom-call | tf_op jit(solution)/shard_map/pallas_call | solution.py:254
  (5 shorter events, 0.0 us)
Async XLA Ops:
  6.6 6.4 %copy-start = (s32[16,512]{1,0:T(8,128)S(1)}, s32[16,512]{1,0:T(8,128)}, u32[]{:S(2)}) copy-start(s32[16,512]{1,0:T(8,128)} %param.9) | copy-start | bytes 98308
  6.6 6.4 %copy-start.1 = (s32[16,512]{1,0:T(8,128)S(1)}, s32[16,512]{1,0:T(8,128)}, u32[]{:S(2)}) copy-start(s32[16,512]{1,0:T(8,128)} %param.8) | copy-start | bytes 98308
  6.6 6.4 %copy-start.2 = (s32[16,512]{1,0:T(8,128)S(1)}, s32[16,512]{1,0:T(8,128)}, u32[]{:S(2)}) copy-start(s32[16,512]{1,0:T(8,128)} %param.7) | copy-start | bytes 98308
  6.6 22.2 %all-to-all-start = ((bf16[8,2,64,512]{3,2,1,0:T(8,128)(2,1)}), bf16[8,2,64,512]{3,2,1,0:T(8,128)(2,1)S(1)}, u32[]{:S(2)}, u32[]{:S(2)}) async-start(bf16[8,2,64,512]{3,2,1,0:T(8,128)(2,1)} %get-tuple-element.4), calls=%async_computation | async-start | bytes 2097152 | tf_op jit(solution)/shard_map/all_to_all | solution.py:266
  13.0 6.2 %collective-permute-start.1 = (s32[3,8,512]{2,1,0:T(8,128)S(1)}, s32[3,8,512]{2,1,0:T(8,128)S(1)}, u32[]{:S(2)}, u32[]{:S(2)}) collective-permute-start(s32[3,8,512]{2,1,0:T(8,128)S(1)} %get-tuple-element.8), channel_id=1, source_target_pairs={{0,1},{1,0},{2,3},{3,2},{4,5},{5,4},{6,7},{7,6},{8,9},{9,8},{10,11... | collective-permute-start | bytes 147464 | tf_op jit(solution)/shard_map/ppermute | solution.py:211
  14.1 5.7 %collective-permute-start = (s32[3,8,512]{2,1,0:T(8,128)S(1)}, s32[3,8,512]{2,1,0:T(8,128)S(1)}, u32[]{:S(2)}, u32[]{:S(2)}) collective-permute-start(s32[3,8,512]{2,1,0:T(8,128)S(1)} %get-tuple-element.9), channel_id=1, source_target_pairs={{1,2},{2,1},{3,4},{4,3},{5,6},{6,5},{7,8},{8,7},{9,10},{10,9},{11,... | collective-permute-start | bytes 147464 | tf_op jit(solution)/shard_map/ppermute | solution.py:212
